TPU v7x, 32 devices: a whole 2x2x4 slice. The times are simulated.
32 devices in a mesh: beam: 8 (over y, x, core), trans: 4 (over z).
Axes of the slice: x: 2, y: 2, z: 4, core: 2. Of those that a mesh axis runs over, the one named last changes fastest.
Arguments:
- field_in: float32 [2, 32, 256, 256], P(None, 'beam', 'trans'), may hold values from -4 to 4
- phases: float32 [32, 4096], P('beam'), may hold values from -3.140625 to 3.140625
- energy: float32 [32, 4096], P('beam'), may hold values from -3 to 3
- row_cell: int32 [32, 4096], P('beam'), may hold values from 32 to 223
- col_cell: int32 [32, 4096], P('beam'), may hold values from 32 to 223
- weight: int32 [32, 4096], P('beam'), may hold values from 1 to 15
- charge: int32 [32], P('beam'), may hold values from 256 to 1024
- pole_rate: float32 [8], replicated, may hold values from 0.0078125 to 0.5
- pole_freq: float32 [8], replicated, may hold values from 0 to 0.3
- pole_amp: float32 [8], replicated, may hold values from -3 to 3
Outputs:
- field_out: float32 [2, 32, 256, 256], P(None, 'beam', 'trans')
- phase_out: float32 [32, 4096], P('beam')
- energy_out: float32 [32, 4096], P('beam')
All inputs are finite; a program needn't handle non-finite values.
Results may differ from a plain program's by a relative error of at most 0.00042.
Values sent between devices are 32-bit elements; how exact they have to be, the bound alone decides.
A program may use at most 64 MiB of HBM per device.

v0:
```python
import functools
import math

import jax
import jax.numpy as jnp
from jax import lax
from jax.sharding import PartitionSpec as P

PERIODS = 2


diffraction = 20.0
kick_gain = 0.5
deposit_gain = 0.05
wake_gain = 3.0
charge_unit = 1024.0


def shifted(value, axis, steps):
    count = lax.axis_size(axis)
    first, last = (max(0, -steps), min(count, count - steps))
    return lax.ppermute(value, axis, [(source, source + steps) for source in range(first, last)])


def complex_product(form, left_re, left_im, right_re, right_im):

    def single(first, second):
        return jnp.einsum(form, first, second, precision=lax.Precision.HIGHEST)

    return (
        single(left_re, right_re) - single(left_im, right_im),
        single(left_re, right_im) + single(left_im, right_re),
    )


def dft_table(length, sign):
    counter = jnp.arange(length, dtype=jnp.int32)
    product = counter[:, None] * counter[None, :] % length
    radians = 2.0 * math.pi / length * product.astype(jnp.float32)
    factor = 1.0 / math.sqrt(length)
    return (jnp.cos(radians) * factor, sign * jnp.sin(radians) * factor)


def propagator(row_index, col_index, length):

    def centred(index):
        return ((index + length // 2) % length - length // 2).astype(jnp.float32) / length

    radians = diffraction * (centred(row_index) ** 2 + centred(col_index) ** 2)
    return (jnp.cos(radians), -jnp.sin(radians))


def pole_power(steps, pole_rate, pole_freq):
    damping = jnp.exp(-pole_rate * steps)
    radians = pole_freq * steps
    return (damping * jnp.cos(radians), damping * jnp.sin(radians))


def wake_kicks(charge, pole_rate, pole_freq, pole_amp):
    members = charge.shape[0]
    groups = lax.axis_size("beam")
    position = lax.axis_index("beam")
    charge_norm = charge.astype(jnp.float32) / charge_unit
    offsets = jnp.arange(members, dtype=jnp.float32)
    distance = offsets[:, None] - offsets[None, :]
    inner_re, inner_im = pole_power(jnp.maximum(distance, 0.0)[..., None], pole_rate, pole_freq)
    before = (distance > 0.0)[..., None]
    local_re = jnp.sum(jnp.where(before, inner_re, 0.0) * charge_norm[None, :, None], axis=1)
    tail_re, tail_im = pole_power((members - offsets)[:, None], pole_rate, pole_freq)
    block_re = jnp.sum(charge_norm[:, None] * tail_re, axis=0)
    block_im = jnp.sum(charge_norm[:, None] * tail_im, axis=0)
    gathered_re, gathered_im = (
        lax.all_gather(block_re[None, :], "beam", axis=0, tiled=True),
        lax.all_gather(block_im[None, :], "beam", axis=0, tiled=True),
    )
    sources = jnp.arange(groups, dtype=jnp.int32)
    spacing = (position - 1 - sources).astype(jnp.float32) * members
    reach_re, reach_im = pole_power(jnp.maximum(spacing, 0.0)[:, None], pole_rate, pole_freq)
    valid = (sources < position)[:, None]
    carry_re = jnp.sum(
        jnp.where(valid, gathered_re * reach_re - gathered_im * reach_im, 0.0), axis=0
    )
    carry_im = jnp.sum(
        jnp.where(valid, gathered_re * reach_im + gathered_im * reach_re, 0.0), axis=0
    )
    lead_re, lead_im = pole_power(offsets[:, None], pole_rate, pole_freq)
    state_re = local_re + lead_re * carry_re[None, :] - lead_im * carry_im[None, :]
    summed = jnp.sum(pole_amp[None, :] * (state_re + 0.5 * charge_norm[:, None]), axis=1)
    return wake_gain / (members * groups) * summed


def deposit_slice(band_rows, grid_cols, operands):
    local_row, column, part_re, part_im = operands
    row_hot = (local_row[:, None] == jnp.arange(band_rows, dtype=jnp.int32)[None, :]).astype(
        jnp.bfloat16
    )
    col_hot = (column[:, None] == jnp.arange(grid_cols, dtype=jnp.int32)[None, :]).astype(
        jnp.bfloat16
    )
    spread = jnp.concatenate([col_hot * part_re[:, None], col_hot * part_im[:, None]], axis=1)
    return lax.dot_general(
        row_hot, spread, (((0,), (0,)), ((), ())), preferred_element_type=jnp.float32
    )


def probe_slice(band_rows, grid_cols, operands):
    local_row, column, slab_re, slab_im = operands
    row_hot = (local_row[:, None] == jnp.arange(band_rows, dtype=jnp.int32)[None, :]).astype(
        jnp.float32
    )
    stacked = jnp.concatenate([slab_re, slab_im], axis=1)
    picked = jnp.dot(
        row_hot, stacked, precision=lax.Precision.HIGHEST, preferred_element_type=jnp.float32
    )
    col_hot = column[:, None] == jnp.arange(grid_cols, dtype=jnp.int32)[None, :]
    value_re = jnp.sum(jnp.where(col_hot, picked[:, :grid_cols], 0.0), axis=1)
    value_im = jnp.sum(jnp.where(col_hot, picked[:, grid_cols:], 0.0), axis=1)
    return (value_re, value_im)


def diffract(field_re, field_im, forward, inverse):
    cols_re, cols_im = complex_product("srn,nc->scr", field_re, field_im, forward[0], forward[1])
    halves = lax.all_to_all(
        jnp.stack([cols_re, cols_im]), "trans", split_axis=2, concat_axis=3, tiled=True
    )
    part_re = halves[0]
    part_im = halves[1]
    col_band = part_re.shape[1]
    grid_rows = part_re.shape[2]
    columns = lax.axis_index("trans") * col_band + jnp.arange(col_band, dtype=jnp.int32)
    spec_re, spec_im = complex_product("sqr,rk->sqk", part_re, part_im, forward[0], forward[1])
    kernel_re, kernel_im = propagator(
        jnp.arange(grid_rows, dtype=jnp.int32)[None, :], columns[:, None], grid_rows
    )
    moved_re = spec_re * kernel_re - spec_im * kernel_im
    moved_im = spec_re * kernel_im + spec_im * kernel_re
    back_re, back_im = complex_product("sqk,kr->sqr", moved_re, moved_im, inverse[0], inverse[1])
    rows_both = lax.all_to_all(
        jnp.stack([back_re, back_im]), "trans", split_axis=3, concat_axis=2, tiled=True
    )
    return complex_product("scr,cn->srn", rows_both[0], rows_both[1], inverse[0], inverse[1])


def shards(
    field_in, phases, energy, row_cell, col_cell, weight, charge, pole_rate, pole_freq, pole_amp
):
    field_re = field_in[0]
    field_im = field_in[1]
    slab_count, band_rows, grid_cols = field_re.shape
    row_start = lax.axis_index("trans") * band_rows
    wake_kick = wake_kicks(charge, pole_rate, pole_freq, pole_amp)
    charge_norm = charge.astype(jnp.float32) / charge_unit
    strength = (deposit_gain * charge_norm)[:, None, None]
    local_row = row_cell - row_start
    weights = weight.astype(jnp.float32)
    forward = dft_table(grid_cols, -1.0)
    inverse = dft_table(grid_cols, 1.0)
    depositor = functools.partial(deposit_slice, band_rows, grid_cols)
    reader = functools.partial(probe_slice, band_rows, grid_cols)
    angles = phases
    energies = energy
    for period in range(PERIODS):
        local_re, local_im = lax.map(reader, (local_row, col_cell, field_re, field_im))
        probed = lax.psum(jnp.stack([local_re, local_im]), "trans")
        energies = (
            energies
            - kick_gain * (probed[0] * jnp.cos(angles) - probed[1] * jnp.sin(angles))
            - wake_kick[:, None]
        )
        angles = angles + energies
        part_re = (weights * jnp.cos(angles)).astype(jnp.bfloat16)
        part_im = (-weights * jnp.sin(angles)).astype(jnp.bfloat16)
        bunched = lax.map(depositor, (local_row, col_cell, part_re, part_im))
        field_re = field_re + strength * bunched[:, :, :grid_cols]
        field_im = field_im + strength * bunched[:, :, grid_cols:]
        field_re, field_im = diffract(field_re, field_im, forward, inverse)
        head_slice = shifted(jnp.stack([field_re[-1], field_im[-1]]), "beam", 1)
        field_re = jnp.concatenate([head_slice[0][None], field_re[:-1]], axis=0)
        field_im = jnp.concatenate([head_slice[1][None], field_im[:-1]], axis=0)
    return (jnp.stack([field_re, field_im]), angles, energies)


def solution(mesh):
    placed = (
        P(None, "beam", "trans", None),
        P("beam", None),
        P("beam", None),
        P("beam", None),
        P("beam", None),
        P("beam", None),
        P("beam"),
        P(),
        P(),
        P(),
    )
    return jax.shard_map(
        shards,
        mesh=mesh,
        in_specs=placed,
        out_specs=(P(None, "beam", "trans", None), P("beam", None), P("beam", None)),
        check_vma=False,
    )
```

profile of v0, /device:TPU:4, one launch (start us, length us, event | category | flops | bytes accessed | tf_op | source)
XLA Modules:
  0.0 326.4 jit_solution(15539974709378980100)
XLA Ops:
  9.3 24.3 %while.44 = (s32[]{:T(128)}, f32[4,4096]{1,0:T(4,128)S(1)}, f32[4,4096]{1,0:T(4,128)S(1)}, s32[4,4096]{1,0:T(4,128)}, s32[4,4096]{1,0:T(4,128)S(1)}, /*index=5*/...) while((s32[]{:T(128)}, f32[4,4096]{1,0:T(4,128)S(1)}, f32[4,4096]{1,0:T(4,128)S(1)}, ...), condition=%wide.region_3.4_spmd, body=%wide.region_0.3_spmd.sunk | while | flops 1616142336 | bytes 17367148 | solution.py:163
  10.2 3.7 %fusion.386 = f32[4096,512]{0,1:T(8,128)S(1)} fusion(s32[4096]{0:T(1024)S(1)} %bitcast.276, f32[64,256]{1,0:T(8,128)S(1)} %get-tuple-element.425, f32[64,256]{1,0:T(8,128)S(1)} %get-tuple-element.426), kind=kOutput, calls=%fused_computation.6.clone.1 | convolution fusion | flops 1610907648 | bytes 8536064 | tf_op jit(solution)/shard_map/while/body/eval_jaxpr/dot_general | solution.py:112
  16.3 3.7 %fusion.386 = f32[4096,512]{0,1:T(8,128)S(1)} fusion(s32[4096]{0:T(1024)S(1)} %bitcast.276, f32[64,256]{1,0:T(8,128)S(1)} %get-tuple-element.425, f32[64,256]{1,0:T(8,128)S(1)} %get-tuple-element.426), kind=kOutput, calls=%fused_computation.6.clone.1 | convolution fusion | flops 1610907648 | bytes 8536064 | tf_op jit(solution)/shard_map/while/body/eval_jaxpr/dot_general | solution.py:112
  22.4 3.7 %fusion.386 = f32[4096,512]{0,1:T(8,128)S(1)} fusion(s32[4096]{0:T(1024)S(1)} %bitcast.276, f32[64,256]{1,0:T(8,128)S(1)} %get-tuple-element.425, f32[64,256]{1,0:T(8,128)S(1)} %get-tuple-element.426), kind=kOutput, calls=%fused_computation.6.clone.1 | convolution fusion | flops 1610907648 | bytes 8536064 | tf_op jit(solution)/shard_map/while/body/eval_jaxpr/dot_general | solution.py:112
  28.4 3.7 %fusion.386 = f32[4096,512]{0,1:T(8,128)S(1)} fusion(s32[4096]{0:T(1024)S(1)} %bitcast.276, f32[64,256]{1,0:T(8,128)S(1)} %get-tuple-element.425, f32[64,256]{1,0:T(8,128)S(1)} %get-tuple-element.426), kind=kOutput, calls=%fused_computation.6.clone.1 | convolution fusion | flops 1610907648 | bytes 8536064 | tf_op jit(solution)/shard_map/while/body/eval_jaxpr/dot_general | solution.py:112
  36.2 12.8 %all-reduce.2 = (f32[64]{0:T(128)S(1)}, f32[64]{0:T(128)S(1)}) all-reduce(f32[64]{0:T(128)S(1)} %dynamic-update-slice.1, f32[64]{0:T(128)S(1)} %dynamic-update-slice), channel_id=3, replica_groups=mesh['beam'=8,'trans'=4] {'beam'}, use_global_device_ids=true, to_apply=%add.1 | all-reduce | flops 128 | bytes 1024
  49.7 20.4 %all-reduce.6.cloned.1.call-done = f32[2,4,4096]{2,1,0:T(4,128)} async-done(((f32[2,4,4096]{2,1,0:T(4,128)}), f32[2,4,4096]{2,1,0:T(4,128)}) %all-reduce.6.cloned.1.call-update) | async-done | bytes 131088 | tf_op jit(solution)/shard_map/psum | solution.py:164
  70.0 1.8 fusion.349
  72.4 22.7 %while.45 = (s32[]{:T(128)}, f32[4,64,512]{2,1,0:T(8,128)S(1)}, s32[4,4096]{1,0:T(4,128)S(1)}, s32[4,4096]{1,0:T(4,128)}, bf16[4,4096]{1,0:T(4,128)(2,1)S(1)}, /*index=5*/bf16[4,4096]{1,0:T(4,128)(2,1)S(1)}, s32[]{:T(128)}) while((s32[]{:T(128)}, f32[4,64,512]{2,1,0:T(8,128)S(1)}, s32[4,4096]{1,0:T(4,128)S(1)}, s32[4,4096]{1,0:T(4,128)}, ...), condition=%wide.region_12.13_spmd, body=%wide.region_11.12_spmd.sunk | while | flops 280231936 | bytes 8667225 | solution.py:173
  73.5 3.2 fusion.389
  76.7 1.4 fusion.390
  79.1 3.2 fusion.389
  82.3 1.4 fusion.390
  84.8 3.2 fusion.389
  88.0 1.4 fusion.390
  90.4 3.2 fusion.389
  93.6 1.4 fusion.390
  95.1 1.4 fusion.101
  96.5 1.4 fusion.76
  97.9 1.4 fusion.51
  99.3 1.4 fusion.50
  101.2 1.8 reshape.236
  103.0 3.5 %all-to-all-start = ((f32[4,1,32768]{2,1,0:T(1,128)}), f32[4,1,32768]{2,1,0:T(1,128)S(1)}, u32[]{:S(2)}, u32[]{:S(2)}) async-start(f32[4,1,32768]{2,1,0:T(1,128)} %reshape.236), calls=%async_computation | async-start | bytes 1048576 | tf_op jit(solution)/shard_map/all_to_all | solution.py:123
  107.3 11.9 %all-to-all-done = f32[4,1,32768]{2,1,0:T(1,128)S(1)} async-done(((f32[4,1,32768]{2,1,0:T(1,128)}), f32[4,1,32768]{2,1,0:T(1,128)S(1)}, u32[]{:S(2)}, u32[]{:S(2)}) %all-to-all-start) | async-done | bytes 524320 | tf_op jit(solution)/shard_map/all_to_all | solution.py:123
  119.7 2.1 reduce.8
  129.4 1.4 fusion.95
  130.8 1.6 fusion.64
  132.3 1.4 fusion.49
  136.6 15.5 %all_to_all.60 = f32[4,1,32768]{2,1,0:T(1,128)S(1)} all-to-all(f32[4,1,32768]{2,1,0:T(1,128)S(1)} %reshape.238), channel_id=1, replica_groups=mesh['beam'=8,'trans'=4] {'trans'}, dimensions={0} | all-to-all | bytes 1048576 | tf_op jit(solution)/shard_map/all_to_all | solution.py:138
  152.1 2.1 reduce.9
  160.5 1.4 convolution_subtract_fusion.4
  161.9 2.1 collective-permute-start
  164.1 5.0 %collective-permute-done = f32[2,64,256]{2,1,0:T(8,128)S(1)} collective-permute-done((f32[2,64,256]{2,1,0:T(8,128)S(1)}, f32[2,64,256]{2,1,0:T(8,128)S(1)}, u32[]{:S(2)}, u32[]{:S(2)}) %collective-permute-start) | collective-permute-done | bytes 131104 | tf_op jit(solution)/shard_map/ppermute | solution.py:22
  169.2 20.9 %while.46 = (s32[]{:T(128)}, f32[4,4096]{1,0:T(4,128)S(1)}, f32[4,4096]{1,0:T(4,128)S(1)}, s32[4,4096]{1,0:T(4,128)S(1)}, s32[4,4096]{1,0:T(4,128)S(1)}, /*index...) while((s32[]{:T(128)}, f32[4,4096]{1,0:T(4,128)S(1)}, ...), condition=%wide.region_16.17_spmd, body=%wide.region_13.16_spmd.sunk | while | flops 1616142336 | bytes 17367148 | solution.py:163
  169.3 3.7 %fusion.392 = f32[4096,512]{0,1:T(8,128)S(1)} fusion(s32[4096]{0:T(1024)S(1)} %bitcast.277, f32[64,256]{1,0:T(8,128)S(1)} %get-tuple-element.450, f32[64,256]{1,0:T(8,128)S(1)} %get-tuple-element.451), kind=kOutput, calls=%fused_computation.22.clone.1 | convolution fusion | flops 1610907648 | bytes 8536064 | tf_op jit(solution)/shard_map/while/body/eval_jaxpr/dot_general | solution.py:112
  174.5 3.7 %fusion.392 = f32[4096,512]{0,1:T(8,128)S(1)} fusion(s32[4096]{0:T(1024)S(1)} %bitcast.277, f32[64,256]{1,0:T(8,128)S(1)} %get-tuple-element.450, f32[64,256]{1,0:T(8,128)S(1)} %get-tuple-element.451), kind=kOutput, calls=%fused_computation.22.clone.1 | convolution fusion | flops 1610907648 | bytes 8536064 | tf_op jit(solution)/shard_map/while/body/eval_jaxpr/dot_general | solution.py:112
  179.7 3.7 %fusion.392 = f32[4096,512]{0,1:T(8,128)S(1)} fusion(s32[4096]{0:T(1024)S(1)} %bitcast.277, f32[64,256]{1,0:T(8,128)S(1)} %get-tuple-element.450, f32[64,256]{1,0:T(8,128)S(1)} %get-tuple-element.451), kind=kOutput, calls=%fused_computation.22.clone.1 | convolution fusion | flops 1610907648 | bytes 8536064 | tf_op jit(solution)/shard_map/while/body/eval_jaxpr/dot_general | solution.py:112
  184.9 3.7 %fusion.392 = f32[4096,512]{0,1:T(8,128)S(1)} fusion(s32[4096]{0:T(1024)S(1)} %bitcast.277, f32[64,256]{1,0:T(8,128)S(1)} %get-tuple-element.450, f32[64,256]{1,0:T(8,128)S(1)} %get-tuple-element.451), kind=kOutput, calls=%fused_computation.22.clone.1 | convolution fusion | flops 1610907648 | bytes 8536064 | tf_op jit(solution)/shard_map/while/body/eval_jaxpr/dot_general | solution.py:112
  190.8 32.7 %all-reduce.8.cloned.1.call-done = f32[2,4,4096]{2,1,0:T(4,128)} async-done(((f32[2,4,4096]{2,1,0:T(4,128)}), f32[2,4,4096]{2,1,0:T(4,128)}) %all-reduce.8.cloned.1.call-update) | async-done | bytes 131088 | tf_op jit(solution)/shard_map/psum | solution.py:164
  223.5 2.0 multiply_convert_fusion
  226.1 19.7 %while.47 = (s32[]{:T(128)}, f32[4,64,512]{2,1,0:T(8,128)S(1)}, s32[4,4096]{1,0:T(4,128)S(1)}, s32[4,4096]{1,0:T(4,128)S(1)}, bf16[4,4096]{1,0:T(4,128)(2,1)S(1)}, /*index=5*/bf16[4,4096]{1,0:T(4,128)(2,1)S(1)}, s32[]{:T(128)}) while((s32[]{:T(128)}, f32[4,64,512]{2,1,0:T(8,128)S(1)}, s32[4,4096]{1,0:T(4,128)S(1)}, ...), condition=%wide.region_19.20_spmd, body=%wide.region_18.19_spmd.sunk | while | flops 280231936 | bytes 8667225 | solution.py:173
  226.3 3.2 fusion.395
  229.5 1.4 fusion.396
  231.1 3.2 fusion.395
  234.3 1.4 fusion.396
  235.9 3.2 fusion.395
  239.1 1.4 fusion.396
  240.7 3.2 fusion.395
  243.9 1.4 fusion.396
  245.8 1.4 fusion.71
  247.2 1.4 fusion.88
  248.6 1.4 fusion.47
  250.0 1.4 fusion.46
  252.9 15.8 %all_to_all.61 = f32[4,1,32768]{2,1,0:T(1,128)S(1)} all-to-all(f32[4,1,32768]{2,1,0:T(1,128)S(1)} %reshape.240), channel_id=1, replica_groups=mesh['beam'=8,'trans'=4] {'trans'}, dimensions={0} | all-to-all | bytes 1048576 | tf_op jit(solution)/shard_map/all_to_all | solution.py:123
  268.7 2.1 reduce.10
  274.0 1.4 fusion.67
  279.8 1.6 fusion.58
  281.4 1.4 fusion.45
  282.8 1.4 fusion.44
  285.7 15.8 %all_to_all.62 = f32[4,1,32768]{2,1,0:T(1,128)S(1)} all-to-all(f32[4,1,32768]{2,1,0:T(1,128)S(1)} %reshape.242), channel_id=1, replica_groups=mesh['beam'=8,'trans'=4] {'trans'}, dimensions={0} | all-to-all | bytes 1048576 | tf_op jit(solution)/shard_map/all_to_all | solution.py:138
  301.5 2.1 reduce.11
  308.5 1.4 convolution_subtract_fusion
  311.3 1.9 collective-permute-start.1
  313.2 5.2 %collective-permute-done.1 = f32[2,64,256]{2,1,0:T(8,128)S(1)} collective-permute-done((f32[2,64,256]{2,1,0:T(8,128)S(1)}, f32[2,64,256]{2,1,0:T(8,128)S(1)}, u32[]{:S(2)}, u32[]{:S(2)}) %collective-permute-start.1) | collective-permute-done | bytes 131104 | tf_op jit(solution)/shard_map/ppermute | solution.py:22
  (180 shorter events, 62.4 us)
Async XLA Ops:
  7.2 62.9 %all-reduce.6.cloned.1.call-start = ((), (), s32[]{:S(2)}) async-start(), calls=%async_computation.4 | async-start | bytes 262144 | tf_op jit(solution)/shard_map/psum | solution.py:164
  9.2 25.1 %copy-start.7 = (s32[4]{0:T(128)S(1)}, s32[4]{0:T(128)}, u32[]{:S(2)}) copy-start(s32[4]{0:T(128)} %param.24) | copy-start | bytes 52
  9.2 25.1 %copy-start.9 = (f32[8]{0:T(128)S(1)}, f32[8]{0:T(128)}, u32[]{:S(2)}) copy-start(f32[8]{0:T(128)} %param.25) | copy-start | bytes 100
  9.2 25.1 %copy-start.10 = (u32[32]{0:T(128)S(1)}, u32[32]{0:T(128)}, u32[]{:S(2)}) copy-start(u32[32]{0:T(128)} %constant.163) | copy-start | bytes 388
  9.2 26.4 %copy-start.6 = (f32[8]{0:T(128)S(1)}, f32[8]{0:T(128)}, u32[]{:S(2)}) copy-start(f32[8]{0:T(128)} %param.26) | copy-start | bytes 100
  9.2 40.2 %copy-start.8 = (f32[8]{0:T(128)S(1)}, f32[8]{0:T(128)}, u32[]{:S(2)}) copy-start(f32[8]{0:T(128)} %param.27) | copy-start | bytes 100
  9.3 60.8 %copy-start.4 = (f32[4,4096]{1,0:T(4,128)S(1)}, f32[4,4096]{1,0:T(4,128)}, u32[]{:S(2)}) copy-start(f32[4,4096]{1,0:T(4,128)} %param.19) | copy-start | bytes 196612
  9.3 60.8 %copy-start.5 = (f32[4,4096]{1,0:T(4,128)S(1)}, f32[4,4096]{1,0:T(4,128)}, u32[]{:S(2)}) copy-start(f32[4,4096]{1,0:T(4,128)} %param.20) | copy-start | bytes 196612
  9.3 63.0 %copy-start.1 = (s32[4,4096]{1,0:T(4,128)S(1)}, s32[4,4096]{1,0:T(4,128)}, u32[]{:S(2)}) copy-start(s32[4,4096]{1,0:T(4,128)} %param.23) | copy-start | bytes 196612
  72.4 22.7 %copy-start.2 = (f32[2,4,64,256]{3,2,1,0:T(8,128)S(1)}, f32[2,4,64,256]{3,2,1,0:T(8,128)}, u32[]{:S(2)}) copy-start(f32[2,4,64,256]{3,2,1,0:T(8,128)} %param.18) | copy-start | bytes 1572868
  103.0 16.2 %all-to-all-start = ((f32[4,1,32768]{2,1,0:T(1,128)}), f32[4,1,32768]{2,1,0:T(1,128)S(1)}, u32[]{:S(2)}, u32[]{:S(2)}) async-start(f32[4,1,32768]{2,1,0:T(1,128)} %reshape.236), calls=%async_computation | async-start | bytes 1048576 | tf_op jit(solution)/shard_map/all_to_all | solution.py:123
  106.5 117.0 %all-reduce.8.cloned.1.call-start = ((), (), s32[]{:S(2)}) async-start(), calls=%async_computation.5 | async-start | bytes 262144 | tf_op jit(solution)/shard_map/psum | solution.py:164
  156.0 13.2 %copy-start = (s32[4,4096]{1,0:T(4,128)S(1)}, s32[4,4096]{1,0:T(4,128)}, u32[]{:S(2)}) copy-start(s32[4,4096]{1,0:T(4,128)} %get-tuple-element.570) | copy-start | bytes 196612
  161.9 7.2 %collective-permute-start = (f32[2,64,256]{2,1,0:T(8,128)S(1)}, f32[2,64,256]{2,1,0:T(8,128)S(1)}, u32[]{:S(2)}, u32[]{:S(2)}) collective-permute-start(f32[2,64,256]{2,1,0:T(8,128)S(1)} %pad_maximum_fusion.8), channel_id=1, source_target_pairs={{0,4},{4,8},{8,12},{12,16},{16,20},{20,24},{24,28},{1,5},{5,9},{9,... | collective-permute-start | bytes 393224 | tf_op jit(solution)/shard_map/ppermute | solution.py:22
  225.5 0.6 copy-start.3
  311.3 7.2 %collective-permute-start.1 = (f32[2,64,256]{2,1,0:T(8,128)S(1)}, f32[2,64,256]{2,1,0:T(8,128)S(1)}, u32[]{:S(2)}, u32[]{:S(2)}) collective-permute-start(f32[2,64,256]{2,1,0:T(8,128)S(1)} %pad_maximum_fusion.10), channel_id=1, source_target_pairs={{0,4},{4,8},{8,12},{12,16},{16,20},{20,24},{24,28},{1,5},{5,9},{9,... | collective-permute-start | bytes 393224 | tf_op jit(solution)/shard_map/ppermute | solution.py:22
Sparse Core Ops, SparseCore 0:
  34.4 35.5 all-reduce.5
  190.9 32.5 all-reduce.7
where the time goes:
time: 332 us; the launch traced here: 326 us
  matrix products  85.5 us (26%)
  waiting for transfers between devices  75.2 us (23%)
  blocking collectives  59.9 us (18%)
  other arithmetic  49.6 us (15%)
  local copies, waits for them, and re-layouts  31.3 us (9%)
  between operations  15.8 us (5%)
  starting transfers between devices  8.01 us (2%)
    psum x2, waiting for transfers between devices, shards(): probed = lax.psum(jnp.stack([local_re, local_im]), 'trans')  53.1 us
    dot_general x32, matrix products, single(): return jnp.einsum(form, first, second, precision=lax.Precision.HIGHEST)  44.3 us
    all_to_all x2, blocking collectives, diffract(): lax.all_to_all(jnp.stack([back_re, back_im]), 'trans', split_axis=3, conc...  31.3 us
    dot_general x8, matrix products, probe_slice(): jnp.dot(row_hot, stacked, precision=lax.Precision.HIGHEST, preferred_elem...  29.7 us
    mul x8, other arithmetic, deposit_slice(): col_hot * part_re[:, None]  25.6 us
    all_to_all x1, blocking collectives, diffract(): lax.all_to_all(jnp.stack([cols_re, cols_im]), 'trans', split_axis=2, conc...  15.8 us
    unnamed x1, blocking collectives  12.8 us
    all_to_all x1, waiting for transfers between devices, diffract(): lax.all_to_all(jnp.stack([cols_re, cols_im]), 'trans', split_axis=2, conc...  11.9 us
  transfers between devices with their start and end apart: 5, of which 5 were waited for; matrix products, arithmetic and copies ran while one was open for 1% of the time, Pallas kernels for 0%

commit v1 on v0

--- a/solution.py
+++ b/solution.py
@@ -3,7 +3,11 @@
 
 import jax
 import jax.numpy as jnp
+import ml_dtypes
+import numpy as np
 from jax import lax
+from jax.experimental import pallas as pl
+from jax.experimental.pallas import tpu as pltpu
 from jax.sharding import PartitionSpec as P
 
 PERIODS = 2
@@ -180,6 +184,331 @@
     return (jnp.stack([field_re, field_im]), angles, energies)
 
 
+MESH = pl.DeviceIdType.MESH
+LANES = 128
+SUBLANES = 8
+F32 = jnp.float32
+BF16 = jnp.bfloat16
+
+
+def one_axis_propagator(length):
+    index = np.arange(length)
+    centred = ((index + length // 2) % length - length // 2) / length
+    ring = np.fft.ifft(np.exp(-1j * diffraction * centred**2))
+    full = ring[(index[:, None] - index[None, :]) % length]
+    block = np.block([[full.real, -full.imag], [full.imag, full.real]]).astype(np.float32)
+    upper = block.astype(ml_dtypes.bfloat16)
+    lower = (block - upper.astype(np.float32)).astype(ml_dtypes.bfloat16)
+    return np.stack([upper, lower])
+
+
+def two_parts(value):
+    upper = value.astype(BF16)
+    return upper, (value - upper.astype(F32)).astype(BF16)
+
+
+def mm(left, right):
+    return jnp.dot(left, right, preferred_element_type=F32)
+
+
+def mm_t(left, right):
+    return lax.dot_general(left, right, (((1,), (1,)), ((), ())), preferred_element_type=F32)
+
+
+def slices_kernel(
+    groups,
+    field_in, phases, energy, row_cell, col_cell, weight, charge, pole_rate, pole_freq, pole_amp, table,
+    field_out, phase_out, energy_out,
+    field, moved, taps, cells, state, result, arrived, probes, parts, halves, col_hot, row_hot, charges, charge_tile,
+    field_send, field_recv, cell_send, cell_recv, state_send, state_recv, result_send, result_recv,
+    out_send, out_recv, charge_send, charge_recv, local_sems,
+):
+    beam, trans = lax.axis_index("beam"), lax.axis_index("trans")
+    members, band, cols = field_in.shape[1:]
+    rows = members * band
+    total = groups * members
+    width = phases.shape[1] // SUBLANES
+    edge = rows // 8
+    inner = rows - 2 * edge
+    mine = beam * members + trans
+    ahead, behind = lax.rem(beam + 1, groups), lax.rem(beam + groups - 1, groups)
+
+    barrier = pltpu.get_barrier_semaphore()
+
+    def greet(beam_to, trans_to):
+        pl.semaphore_signal(barrier, inc=1, device_id=(beam_to, trans_to), device_id_type=MESH)
+
+    for step in range(1, members):
+        greet(beam, lax.rem(trans + step, members))
+    for step in range(1, groups):
+        greet(lax.rem(beam + step, groups), trans)
+    for source in (members - 2, members - 1):
+        @pl.when(trans != source)
+        def _():
+            greet(behind, source)
+
+    @pl.when(trans == members - 1)
+    def _():
+        greet(ahead, 0)
+
+    take = pltpu.make_async_copy(field_in.at[:, trans], field.at[:, trans], local_sems.at[0])
+    take.start()
+    take_table = pltpu.make_async_copy(table, taps, local_sems.at[1])
+    take_table.start()
+
+    expected = (members - 1) + (groups - 1) + jnp.where(trans >= members - 2, members - 1, 0) + jnp.where(trans == 0, 1, 0)
+    pl.semaphore_wait(barrier, expected)
+
+    def remote(source, target, send, recv, beam_to, trans_to):
+        return pltpu.make_async_remote_copy(
+            src_ref=source, dst_ref=target, send_sem=send, recv_sem=recv,
+            device_id=(beam_to, trans_to), device_id_type=MESH,
+        )
+
+    field_copies = []
+    for step in [members - 1 - k for k in range(members - 1)]:
+        to = lax.rem(trans + step, members)
+        copy = remote(field_in.at[:, to], field.at[:, trans], field_send.at[step], field_recv.at[trans], beam, to)
+        copy.start()
+        field_copies.append(copy)
+
+    lane = lax.broadcasted_iota(jnp.int32, charge_tile.shape, 1)
+    own = jnp.zeros(charge_tile.shape, F32)
+    for k in range(members):
+        own = jnp.where(lane == beam * members + k, charge[k].astype(F32) / charge_unit, own)
+    charge_tile[...] = own
+    charges[pl.ds(beam, 1)] = own[None]
+    charge_copies = []
+    for step in range(1, groups):
+        copy = remote(charge_tile, charges.at[beam], charge_send.at[step], charge_recv.at[beam], lax.rem(beam + step, groups), trans)
+        copy.start()
+        charge_copies.append(copy)
+
+    for k in range(SUBLANES):
+        here = pl.ds(k * width, width)
+        for place, source in enumerate((row_cell, col_cell, weight)):
+            cells[0, place, k : k + 1, :] = source[pl.ds(trans, 1), here].astype(F32)
+        state[0, 0, k : k + 1, :] = phases[pl.ds(trans, 1), here]
+        state[0, 1, k : k + 1, :] = energy[pl.ds(trans, 1), here]
+    first = trans == 0
+    prior_beam = jnp.where(first, behind, beam)
+    prior_trans = jnp.where(first, members - 1, trans - 1)
+    cell_copy = remote(cells.at[0], cells.at[1], cell_send, cell_recv, prior_beam, prior_trans)
+    cell_copy.start()
+
+    def one_hots(period):
+        col_index = lax.broadcasted_iota(jnp.int32, (cols, width), 0).astype(F32)
+
+        def body(k, carry):
+            col_hot[period, k] = jnp.where(cells[period, 1, pl.ds(k, 1), :] == col_index, 1.0, 0.0).astype(BF16)
+            return carry
+
+        lax.fori_loop(0, SUBLANES, body, 0)
+
+    one_hots(0)
+
+    for step in range(1, groups):
+        source = lax.rem(beam + step, groups)
+        remote(charge_tile, charges.at[source], charge_send.at[step], charge_recv.at[source], source, trans).wait_recv()
+    every = jnp.sum(charges[...], axis=0)
+
+    def wake_and_charge(slice_id):
+        distance = slice_id - lane
+        ago = jnp.maximum(distance, 0).astype(F32)
+        memory = jnp.zeros(lane.shape, F32)
+        amount = F32(0)
+        for k in range(pole_rate.shape[0]):
+            memory = memory + pole_amp[k] * (jnp.exp(-pole_rate[k] * ago) * jnp.cos(pole_freq[k] * ago))
+            amount = amount + pole_amp[k]
+        memory = jnp.where(distance > 0, memory, jnp.where(distance == 0, 0.5 * amount, 0.0))
+        wake = (wake_gain / total) * jnp.sum(memory * every, axis=1, keepdims=True)
+        return wake, jnp.sum(jnp.where(distance == 0, every, 0.0), axis=1, keepdims=True)
+
+    following = lax.rem(mine + 1, total)
+    wakes = [wake_and_charge(mine), wake_and_charge(following)]
+    cell_copy.wait_recv()
+    one_hots(1)
+    start_cos, start_sin = jnp.cos(state[0, 0]), jnp.sin(state[0, 0])
+
+    take.wait()
+    for step in range(1, members):
+        source = lax.rem(trans + step, members)
+        remote(field_in.at[:, source], field.at[:, source], field_send.at[step], field_recv.at[source], beam, source).wait_recv()
+    take_table.wait()
+
+    row_index = lax.broadcasted_iota(jnp.int32, (inner, width), 0).astype(F32) + float(edge)
+
+    def push(period, cos_now, sin_now):
+        flat = field[...].reshape(2, rows, cols)
+        for part in range(2):
+            upper, lower = two_parts(flat[part, edge : rows - edge])
+            halves[0, part * inner : (part + 1) * inner, :] = upper
+            halves[1, part * inner : (part + 1) * inner, :] = lower
+
+        def body(k, carry):
+            hot = col_hot[period, k]
+            picked = mm(halves[0], hot) + mm(halves[1], hot)
+            inside = cells[period, 0, pl.ds(k, 1), :] == row_index
+            probes[0, pl.ds(k, 1), :] = jnp.sum(jnp.where(inside, picked[:inner], 0.0), axis=0, keepdims=True)
+            probes[1, pl.ds(k, 1), :] = jnp.sum(jnp.where(inside, picked[inner:], 0.0), axis=0, keepdims=True)
+            return carry
+
+        lax.fori_loop(0, SUBLANES, body, 0, unroll=True)
+        eta = state[period, 1] - kick_gain * (probes[0] * cos_now - probes[1] * sin_now) - wakes[period][0]
+        theta = state[period, 0] + eta
+        return theta, eta
+
+    def deposit_and_diffract(period, theta):
+        heavy = cells[period, 2]
+        parts[0] = (heavy * jnp.cos(theta)).astype(BF16).astype(F32)
+        parts[1] = (-heavy * jnp.sin(theta)).astype(BF16).astype(F32)
+        bunched = jnp.zeros((2 * inner, cols), F32)
+        for k in range(SUBLANES):
+            inside = cells[period, 0, k : k + 1, :] == row_index
+            spread = jnp.concatenate(
+                [jnp.where(inside, parts[part, k : k + 1, :], 0.0).astype(BF16) for part in range(2)], axis=0
+            )
+            row_hot[:, k * width : (k + 1) * width] = spread
+            bunched = bunched + mm_t(row_hot[:, k * width : (k + 1) * width], col_hot[period, k])
+        strength = deposit_gain * wakes[period][1][:1, :1]
+        flat = field[...].reshape(2, rows, cols)
+        wide = []
+        for part in range(2):
+            loaded = flat[part, edge : rows - edge] + strength * bunched[part * inner : (part + 1) * inner]
+            wide.append(jnp.concatenate([flat[part, :edge], loaded, flat[part, rows - edge :]], axis=0))
+        upper, lower = two_parts(jnp.concatenate(wide, axis=1))
+        across = mm_t(upper, taps[0]) + (mm_t(lower, taps[0]) + mm_t(upper, taps[1]))
+        upper, lower = two_parts(jnp.concatenate([across[:, :cols], across[:, cols:]], axis=0))
+        return mm(taps[0], upper) + (mm(taps[0], lower) + mm(taps[1], upper))
+
+    theta, eta = push(0, start_cos, start_sin)
+    state[0, 0] = theta
+    state[0, 1] = eta
+    state_copy = remote(state.at[0], state.at[1], state_send, state_recv, prior_beam, prior_trans)
+    state_copy.start()
+    spread_field = deposit_and_diffract(0, theta)
+    field[...] = jnp.where(following == 0, 0.0, spread_field).reshape(field.shape)
+
+    state_copy.wait_recv()
+    theta, eta = push(1, jnp.cos(state[1, 0]), jnp.sin(state[1, 0]))
+    result[0] = theta
+    result[1] = eta
+
+    def scatter(shift, source_of, target, send, recv, sem):
+        slot = lax.rem(trans + shift, members)
+        stays = trans + shift < members
+        beam_to = jnp.where(stays, beam, ahead)
+        copies = []
+        for step in [members // 2 + k for k in range(members - members // 2)] + list(range(1, members // 2)):
+            to = lax.rem(trans + step, members)
+            copy = remote(source_of(to), target(slot), send.at[step], recv.at[slot], beam_to, to)
+            copy.start()
+            copies.append(copy)
+        away = remote(source_of(trans), target(slot), send.at[0], recv.at[slot], ahead, trans)
+        here = pltpu.make_async_copy(source_of(trans), target(slot), sem)
+
+        @pl.when(stays)
+        def _():
+            here.start()
+
+        @pl.when(jnp.logical_not(stays))
+        def _():
+            away.start()
+
+        def finish():
+            for copy in copies:
+                copy.wait_send()
+
+            @pl.when(stays)
+            def _():
+                here.wait()
+
+            @pl.when(jnp.logical_not(stays))
+            def _():
+                away.wait_send()
+
+            for place in range(members):
+                def wait_for():
+                    remote(source_of(trans), target(place), send.at[0], recv.at[place], beam, trans).wait_recv()
+
+                if place < shift:
+                    wait_for()
+                else:
+                    pl.when(trans != place - shift)(wait_for)
+
+        return finish
+
+    finish_result = scatter(
+        1, lambda to: result, lambda slot: arrived.at[slot], result_send, result_recv, local_sems.at[2]
+    )
+    spread_field = deposit_and_diffract(1, theta)
+    moved[...] = jnp.where(lax.rem(mine + 2, total) == 0, 0.0, spread_field).reshape(moved.shape)
+    finish_field = scatter(
+        2, lambda to: moved.at[:, to], lambda slot: field_out.at[:, slot], out_send, out_recv, local_sems.at[3]
+    )
+
+    finish_result()
+    for place in range(members):
+        for k in range(SUBLANES):
+            here = slice(k * width, (k + 1) * width)
+            phase_out[place : place + 1, here] = arrived[place, 0, k : k + 1, :]
+            energy_out[place : place + 1, here] = arrived[place, 1, k : k + 1, :]
+    for copy in field_copies + charge_copies + [cell_copy, state_copy]:
+        copy.wait_send()
+    finish_field()
+
+
+def whole_slices(
+    field_in, phases, energy, row_cell, col_cell, weight, charge, pole_rate, pole_freq, pole_amp
+):
+    groups, members = lax.axis_size("beam"), lax.axis_size("trans")
+    band, cols = field_in.shape[2:]
+    rows = members * band
+    inner = rows - 2 * (rows // 8)
+    width = phases.shape[1] // SUBLANES
+    lanes = -(-groups * members // LANES) * LANES
+    table = jnp.asarray(one_axis_propagator(cols))
+    vmem, smem, anywhere = (pl.BlockSpec(memory_space=space) for space in (pltpu.VMEM, pltpu.SMEM, pl.ANY))
+    dma = pltpu.SemaphoreType.DMA
+    return tuple(pl.pallas_call(
+        functools.partial(slices_kernel, groups),
+        out_shape=(
+            jax.ShapeDtypeStruct(field_in.shape, F32),
+            jax.ShapeDtypeStruct(phases.shape, F32),
+            jax.ShapeDtypeStruct(energy.shape, F32),
+        ),
+        in_specs=[anywhere] + [vmem] * 5 + [smem] * 4 + [anywhere],
+        out_specs=(anywhere, vmem, vmem),
+        scratch_shapes=[
+            pltpu.VMEM((2, members, band, cols), F32),
+            pltpu.VMEM((2, members, band, cols), F32),
+            pltpu.VMEM(table.shape, BF16),
+            pltpu.VMEM((2, 3, SUBLANES, width), F32),
+            pltpu.VMEM((2, 2, SUBLANES, width), F32),
+            pltpu.VMEM((2, SUBLANES, width), F32),
+            pltpu.VMEM((members, 2, SUBLANES, width), F32),
+            pltpu.VMEM((2, SUBLANES, width), F32),
+            pltpu.VMEM((2, SUBLANES, width), F32),
+            pltpu.VMEM((2, 2 * inner, cols), BF16),
+            pltpu.VMEM((2, SUBLANES, cols, width), BF16),
+            pltpu.VMEM((2 * inner, SUBLANES * width), BF16),
+            pltpu.VMEM((groups, SUBLANES, lanes), F32),
+            pltpu.VMEM((SUBLANES, lanes), F32),
+            dma((members,)), dma((members,)), dma, dma, dma, dma, dma((members,)), dma((members,)),
+            dma((members,)), dma((members,)), dma((groups,)), dma((groups,)), dma((4,)),
+        ],
+        compiler_params=pltpu.CompilerParams(
+            collective_id=0, has_side_effects=True, vmem_limit_bytes=40 * 1024 * 1024
+        ),
+    )(field_in, phases, energy, row_cell, col_cell, weight, charge, pole_rate, pole_freq, pole_amp, table))
+
+
+def pick_plan(field_in, *others):
+    members = field_in.shape[1]
+    whole = members == lax.axis_size("trans") and members >= 3 and lax.axis_size("beam") >= 3
+    return (whole_slices if whole else shards)(field_in, *others)
+
+
 def solution(mesh):
     placed = (
         P(None, "beam", "trans", None),
@@ -194,7 +523,7 @@
         P(),
     )
     return jax.shard_map(
-        shards,
+        pick_plan,
         mesh=mesh,
         in_specs=placed,
         out_specs=(P(None, "beam", "trans", None), P("beam", None), P("beam", None)),

time: 332 us -> 56 us (0.17)
  the two profiles are of different devices: /device:TPU:4 before, /device:TPU:0 now
where the time goes in v1:
time: 56 us; the launch traced here: 55.5 us
  Pallas kernels  43.7 us (78%)
  local copies, waits for them, and re-layouts  11.1 us (20%)
  between operations  0.66 us (1%)
    pallas_call x1, Pallas kernels, whole_slices(): pl.pallas_call(functools.partial(slices_kernel, groups), out_shape=(jax.S...  43.7 us
    unnamed x25, local copies, waits for them, and re-layouts  11.1 us

profile of v1, /device:TPU:0, one launch (start us, length us, event | category | flops | bytes accessed | tf_op | source)
XLA Modules:
  0.0 55.5 jit_solution(143654643218184709)
XLA Ops:
  0.6 0.0 copy-start
  0.6 1.2 %copy-done = bf16[2,512,512]{2,1,0:T(8,128)(2,1)S(1)} copy-done((bf16[2,512,512]{2,1,0:T(8,128)(2,1)S(1)}, bf16[2,512,512]{2,1,0:T(8,128)(2,1)}, u32[]{:S(2)}) %copy-start) | copy-done | bytes 1048600
  1.9 0.0 copy-start.1
  1.9 1.0 %copy-done.1 = f32[2,4,64,256]{3,2,1,0:T(8,128)S(1)} copy-done((f32[2,4,64,256]{3,2,1,0:T(8,128)S(1)}, f32[2,4,64,256]{3,2,1,0:T(8,128)}, u32[]{:S(2)}) %copy-start.1) | copy-done | bytes 524312
  2.9 0.0 copy-start.2
  2.9 0.8 %copy-done.2 = f32[4,4096]{1,0:T(4,128)S(1)} copy-done((f32[4,4096]{1,0:T(4,128)S(1)}, f32[4,4096]{1,0:T(4,128)}, u32[]{:S(2)}) %copy-start.2) | copy-done | bytes 65560
  3.7 0.0 copy-start.3
  3.7 0.8 %copy-done.3 = f32[4,4096]{1,0:T(4,128)S(1)} copy-done((f32[4,4096]{1,0:T(4,128)S(1)}, f32[4,4096]{1,0:T(4,128)}, u32[]{:S(2)}) %copy-start.3) | copy-done | bytes 65560
  4.6 0.0 copy-start.4
  4.6 0.8 %copy-done.4 = s32[4,4096]{1,0:T(4,128)S(1)} copy-done((s32[4,4096]{1,0:T(4,128)S(1)}, s32[4,4096]{1,0:T(4,128)}, u32[]{:S(2)}) %copy-start.4) | copy-done | bytes 65560
  5.4 0.0 copy-start.5
  5.4 0.8 %copy-done.5 = s32[4,4096]{1,0:T(4,128)S(1)} copy-done((s32[4,4096]{1,0:T(4,128)S(1)}, s32[4,4096]{1,0:T(4,128)}, u32[]{:S(2)}) %copy-start.5) | copy-done | bytes 65560
  6.3 0.0 copy-start.6
  6.3 0.8 %copy-done.6 = s32[4,4096]{1,0:T(4,128)S(1)} copy-done((s32[4,4096]{1,0:T(4,128)S(1)}, s32[4,4096]{1,0:T(4,128)}, u32[]{:S(2)}) %copy-start.6) | copy-done | bytes 65560
  7.1 0.0 copy-start.7
  7.1 0.7 %copy-done.7 = s32[4]{0:T(128)S(1)} copy-done((s32[4]{0:T(128)S(1)}, s32[4]{0:T(128)}, u32[]{:S(2)}) %copy-start.7) | copy-done | bytes 40
  7.8 0.0 copy-start.8
  7.8 0.7 %copy-done.8 = f32[8]{0:T(128)S(1)} copy-done((f32[8]{0:T(128)S(1)}, f32[8]{0:T(128)}, u32[]{:S(2)}) %copy-start.8) | copy-done | bytes 56
  8.4 0.0 copy-start.9
  8.4 0.7 %copy-done.9 = f32[8]{0:T(128)S(1)} copy-done((f32[8]{0:T(128)S(1)}, f32[8]{0:T(128)}, u32[]{:S(2)}) %copy-start.9) | copy-done | bytes 56
  9.1 0.0 copy-start.10
  9.1 0.7 %copy-done.10 = f32[8]{0:T(128)S(1)} copy-done((f32[8]{0:T(128)S(1)}, f32[8]{0:T(128)}, u32[]{:S(2)}) %copy-start.10) | copy-done | bytes 56
  9.7 43.7 %shard_map.130 = (f32[2,4,64,256]{3,2,1,0:T(8,128)S(1)}, f32[4,4096]{1,0:T(4,128)S(1)}, f32[4,4096]{1,0:T(4,128)S(1)}) custom-call(f32[2,4,64,256]{3,2,1,0:T(8,128)S(1)} %copy-done.1, f32[4,4096]{1,0:T(4,128)S(1)} %copy-done.2, f32[4,4096]{1,0:T(4,128)S(1)} %copy-done.3, s32[4,4096]{1,0:T(4,128)S(1)} %copy-done.4, s32[4,4096]{1,0:T(4,128)S(1)} %copy-done.5, ...), custom_call_target="tpu_custom_call" | custom-call | tf_op jit(solution)/shard_map/pallas_call | solution.py:473
  53.5 0.8 %copy.17 = f32[2,4,64,256]{3,2,1,0:T(8,128)} copy(f32[2,4,64,256]{3,2,1,0:T(8,128)S(1)} %get-tuple-element.6) | data formatting | bytes 1048576
  54.3 0.6 %copy.18 = f32[4,4096]{1,0:T(4,128)} copy(f32[4,4096]{1,0:T(4,128)S(1)} %get-tuple-element.7) | data formatting | bytes 131072
  54.9 0.6 %copy.19 = f32[4,4096]{1,0:T(4,128)} copy(f32[4,4096]{1,0:T(4,128)S(1)} %get-tuple-element.8) | data formatting | bytes 131072
Async XLA Ops:
  0.6 1.2 %copy-start = (bf16[2,512,512]{2,1,0:T(8,128)(2,1)S(1)}, bf16[2,512,512]{2,1,0:T(8,128)(2,1)}, u32[]{:S(2)}) copy-start(bf16[2,512,512]{2,1,0:T(8,128)(2,1)} %constant.2.clone.table) | copy-start | bytes 3145732
  1.9 1.0 %copy-start.1 = (f32[2,4,64,256]{3,2,1,0:T(8,128)S(1)}, f32[2,4,64,256]{3,2,1,0:T(8,128)}, u32[]{:S(2)}) copy-start(f32[2,4,64,256]{3,2,1,0:T(8,128)} %field_in.1) | copy-start | bytes 1572868
  2.9 0.8 %copy-start.2 = (f32[4,4096]{1,0:T(4,128)S(1)}, f32[4,4096]{1,0:T(4,128)}, u32[]{:S(2)}) copy-start(f32[4,4096]{1,0:T(4,128)} %phases.1) | copy-start | bytes 196612
  3.7 0.8 %copy-start.3 = (f32[4,4096]{1,0:T(4,128)S(1)}, f32[4,4096]{1,0:T(4,128)}, u32[]{:S(2)}) copy-start(f32[4,4096]{1,0:T(4,128)} %energy.1) | copy-start | bytes 196612
  4.6 0.8 %copy-start.4 = (s32[4,4096]{1,0:T(4,128)S(1)}, s32[4,4096]{1,0:T(4,128)}, u32[]{:S(2)}) copy-start(s32[4,4096]{1,0:T(4,128)} %row_cell.1) | copy-start | bytes 196612
  5.4 0.8 %copy-start.5 = (s32[4,4096]{1,0:T(4,128)S(1)}, s32[4,4096]{1,0:T(4,128)}, u32[]{:S(2)}) copy-start(s32[4,4096]{1,0:T(4,128)} %col_cell.1) | copy-start | bytes 196612
  6.3 0.8 %copy-start.6 = (s32[4,4096]{1,0:T(4,128)S(1)}, s32[4,4096]{1,0:T(4,128)}, u32[]{:S(2)}) copy-start(s32[4,4096]{1,0:T(4,128)} %weight.1) | copy-start | bytes 196612
  7.1 0.7 %copy-start.7 = (s32[4]{0:T(128)S(1)}, s32[4]{0:T(128)}, u32[]{:S(2)}) copy-start(s32[4]{0:T(128)} %charge.1) | copy-start | bytes 52
  7.8 0.7 %copy-start.8 = (f32[8]{0:T(128)S(1)}, f32[8]{0:T(128)}, u32[]{:S(2)}) copy-start(f32[8]{0:T(128)} %pole_rate.1) | copy-start | bytes 100
  8.4 0.7 %copy-start.9 = (f32[8]{0:T(128)S(1)}, f32[8]{0:T(128)}, u32[]{:S(2)}) copy-start(f32[8]{0:T(128)} %pole_freq.1) | copy-start | bytes 100
  9.1 0.7 %copy-start.10 = (f32[8]{0:T(128)S(1)}, f32[8]{0:T(128)}, u32[]{:S(2)}) copy-start(f32[8]{0:T(128)} %pole_amp.1) | copy-start | bytes 100

commit v2 on v1

--- a/solution.py
+++ b/solution.py
@@ -217,9 +217,9 @@
 
 def slices_kernel(
     groups,
-    field_in, phases, energy, row_cell, col_cell, weight, charge, pole_rate, pole_freq, pole_amp, table,
+    field_in, phases_in, energy_in, row_in, col_in, weight_in, charge_in, rate_in, freq_in, amp_in, table,
     field_out, phase_out, energy_out,
-    field, moved, taps, cells, state, result, arrived, probes, parts, halves, col_hot, row_hot, charges, charge_tile,
+    phases, energy, row_cell, col_cell, weight, charge, pole_rate, pole_freq, pole_amp, field, moved, taps, cells, state, result, arrived, probes, parts, halves, col_hot, row_hot, charges, charge_tile,
     field_send, field_recv, cell_send, cell_recv, state_send, state_recv, result_send, result_recv,
     out_send, out_recv, charge_send, charge_recv, local_sems,
 ):
@@ -227,6 +227,7 @@
     members, band, cols = field_in.shape[1:]
     rows = members * band
     total = groups * members
+    half = members // 2
     width = phases.shape[1] // SUBLANES
     edge = rows // 8
     inner = rows - 2 * edge
@@ -251,6 +252,13 @@
     def _():
         greet(ahead, 0)
 
+    small = []
+    for k, (source, target) in enumerate((
+        (row_in, row_cell), (col_in, col_cell), (weight_in, weight), (phases_in, phases), (energy_in, energy),
+        (charge_in, charge), (rate_in, pole_rate), (freq_in, pole_freq), (amp_in, pole_amp),
+    )):
+        small.append(pltpu.make_async_copy(source, target, local_sems.at[4 + k]))
+        small[-1].start()
     take = pltpu.make_async_copy(field_in.at[:, trans], field.at[:, trans], local_sems.at[0])
     take.start()
     take_table = pltpu.make_async_copy(table, taps, local_sems.at[1])
@@ -266,11 +274,15 @@
         )
 
     field_copies = []
-    for step in [members - 1 - k for k in range(members - 1)]:
-        to = lax.rem(trans + step, members)
+    way = jnp.where(trans < half, 1, members - 1)
+    for step in [half] + [k for k in range(1, members) if k != half]:
+        to = lax.rem(trans + way * step, members)
         copy = remote(field_in.at[:, to], field.at[:, trans], field_send.at[step], field_recv.at[trans], beam, to)
         copy.start()
         field_copies.append(copy)
+
+    for copy in small:
+        copy.wait()
 
     lane = lax.broadcasted_iota(jnp.int32, charge_tile.shape, 1)
     own = jnp.zeros(charge_tile.shape, F32)
@@ -330,15 +342,26 @@
     one_hots(1)
     start_cos, start_sin = jnp.cos(state[0, 0]), jnp.sin(state[0, 0])
 
-    take.wait()
-    for step in range(1, members):
-        source = lax.rem(trans + step, members)
-        remote(field_in.at[:, source], field.at[:, source], field_send.at[step], field_recv.at[source], beam, source).wait_recv()
-    take_table.wait()
-
     row_index = lax.broadcasted_iota(jnp.int32, (inner, width), 0).astype(F32) + float(edge)
 
-    def push(period, cos_now, sin_now):
+    def probe_band(source, opens):
+        upper, lower = two_parts(field[:, source].reshape(2 * band, cols))
+        band_index = (lax.broadcasted_iota(jnp.int32, (band, width), 0) + source * band).astype(F32)
+
+        def body(k, carry):
+            hot = col_hot[0, k]
+            picked = mm(upper, hot) + mm(lower, hot)
+            inside = cells[0, 0, pl.ds(k, 1), :] == band_index
+            for part in range(2):
+                found = jnp.sum(
+                    jnp.where(inside, picked[part * band : (part + 1) * band], 0.0), axis=0, keepdims=True
+                )
+                probes[part, pl.ds(k, 1), :] = found if opens else probes[part, pl.ds(k, 1), :] + found
+            return carry
+
+        lax.fori_loop(0, SUBLANES, body, 0, unroll=True)
+
+    def probe(period):
         flat = field[...].reshape(2, rows, cols)
         for part in range(2):
             upper, lower = two_parts(flat[part, edge : rows - edge])
@@ -354,11 +377,13 @@
             return carry
 
         lax.fori_loop(0, SUBLANES, body, 0, unroll=True)
+
+    def push(period, cos_now, sin_now):
         eta = state[period, 1] - kick_gain * (probes[0] * cos_now - probes[1] * sin_now) - wakes[period][0]
         theta = state[period, 0] + eta
         return theta, eta
 
-    def deposit_and_diffract(period, theta):
+    def deposit(period, theta):
         heavy = cells[period, 2]
         parts[0] = (heavy * jnp.cos(theta)).astype(BF16).astype(F32)
         parts[1] = (-heavy * jnp.sin(theta)).astype(BF16).astype(F32)
@@ -378,18 +403,30 @@
             wide.append(jnp.concatenate([flat[part, :edge], loaded, flat[part, rows - edge :]], axis=0))
         upper, lower = two_parts(jnp.concatenate(wide, axis=1))
         across = mm_t(upper, taps[0]) + (mm_t(lower, taps[0]) + mm_t(upper, taps[1]))
-        upper, lower = two_parts(jnp.concatenate([across[:, :cols], across[:, cols:]], axis=0))
-        return mm(taps[0], upper) + (mm(taps[0], lower) + mm(taps[1], upper))
-
+        return two_parts(jnp.concatenate([across[:, :cols], across[:, cols:]], axis=0))
+
+    def along_rows(first_row, count, upper, lower):
+        here = [pl.ds(pl.multiple_of(part * rows + first_row, band), count) for part in range(2)]
+        major, minor = (jnp.concatenate([taps[part, where] for where in here], axis=0) for part in range(2))
+        return (mm(major, upper) + (mm(major, lower) + mm(minor, upper))).reshape(2, count, cols)
+
+    take.wait()
+    probe_band(trans, True)
+    for step in range(1, members):
+        source = lax.rem(trans + way * step, members)
+        remote(field_in.at[:, source], field.at[:, source], field_send.at[step], field_recv.at[source], beam, source).wait_recv()
+        probe_band(source, False)
+    take_table.wait()
     theta, eta = push(0, start_cos, start_sin)
     state[0, 0] = theta
     state[0, 1] = eta
     state_copy = remote(state.at[0], state.at[1], state_send, state_recv, prior_beam, prior_trans)
     state_copy.start()
-    spread_field = deposit_and_diffract(0, theta)
-    field[...] = jnp.where(following == 0, 0.0, spread_field).reshape(field.shape)
+    turned = along_rows(0, rows, *deposit(0, theta))
+    field[...] = jnp.where(following == 0, 0.0, turned).reshape(field.shape)
 
     state_copy.wait_recv()
+    probe(1)
     theta, eta = push(1, jnp.cos(state[1, 0]), jnp.sin(state[1, 0]))
     result[0] = theta
     result[1] = eta
@@ -398,34 +435,33 @@
         slot = lax.rem(trans + shift, members)
         stays = trans + shift < members
         beam_to = jnp.where(stays, beam, ahead)
-        copies = []
-        for step in [members // 2 + k for k in range(members - members // 2)] + list(range(1, members // 2)):
-            to = lax.rem(trans + step, members)
-            copy = remote(source_of(to), target(slot), send.at[step], recv.at[slot], beam_to, to)
-            copy.start()
-            copies.append(copy)
-        away = remote(source_of(trans), target(slot), send.at[0], recv.at[slot], ahead, trans)
-        here = pltpu.make_async_copy(source_of(trans), target(slot), sem)
-
-        @pl.when(stays)
-        def _():
-            here.start()
-
-        @pl.when(jnp.logical_not(stays))
-        def _():
-            away.start()
+
+        def away(to):
+            return remote(source_of(to), target(slot), send.at[to], recv.at[slot], beam_to, to)
+
+        def here():
+            return pltpu.make_async_copy(source_of(trans), target(slot), sem)
+
+        def start(to):
+            same = jnp.logical_and(stays, to == trans)
+
+            @pl.when(same)
+            def _():
+                here().start()
+
+            @pl.when(jnp.logical_not(same))
+            def _():
+                away(to).start()
 
         def finish():
-            for copy in copies:
-                copy.wait_send()
+            for to in range(members):
+                @pl.when(jnp.logical_not(jnp.logical_and(stays, to == trans)))
+                def _():
+                    away(to).wait_send()
 
             @pl.when(stays)
             def _():
-                here.wait()
-
-            @pl.when(jnp.logical_not(stays))
-            def _():
-                away.wait_send()
+                here().wait()
 
             for place in range(members):
                 def wait_for():
@@ -436,16 +472,24 @@
                 else:
                     pl.when(trans != place - shift)(wait_for)
 
-        return finish
-
-    finish_result = scatter(
+        return start, finish
+
+    start_result, finish_result = scatter(
         1, lambda to: result, lambda slot: arrived.at[slot], result_send, result_recv, local_sems.at[2]
     )
-    spread_field = deposit_and_diffract(1, theta)
-    moved[...] = jnp.where(lax.rem(mine + 2, total) == 0, 0.0, spread_field).reshape(moved.shape)
-    finish_field = scatter(
+    for to in range(members):
+        start_result(to)
+    upper, lower = deposit(1, theta)
+    start_field, finish_field = scatter(
         2, lambda to: moved.at[:, to], lambda slot: field_out.at[:, slot], out_send, out_recv, local_sems.at[3]
     )
+    mine_half = trans // half
+    for side in (1 - mine_half, mine_half):
+        turned = along_rows(side * (half * band), half * band, upper, lower)
+        turned = jnp.where(lax.rem(mine + 2, total) == 0, 0.0, turned)
+        for k in range(half):
+            moved[:, side * half + k] = turned[:, k * band : (k + 1) * band]
+            start_field(side * half + k)
 
     finish_result()
     for place in range(members):
@@ -468,7 +512,7 @@
     width = phases.shape[1] // SUBLANES
     lanes = -(-groups * members // LANES) * LANES
     table = jnp.asarray(one_axis_propagator(cols))
-    vmem, smem, anywhere = (pl.BlockSpec(memory_space=space) for space in (pltpu.VMEM, pltpu.SMEM, pl.ANY))
+    vmem, hbm = (pl.BlockSpec(memory_space=space) for space in (pltpu.VMEM, pltpu.HBM))
     dma = pltpu.SemaphoreType.DMA
     return tuple(pl.pallas_call(
         functools.partial(slices_kernel, groups),
@@ -477,9 +521,11 @@
             jax.ShapeDtypeStruct(phases.shape, F32),
             jax.ShapeDtypeStruct(energy.shape, F32),
         ),
-        in_specs=[anywhere] + [vmem] * 5 + [smem] * 4 + [anywhere],
-        out_specs=(anywhere, vmem, vmem),
+        in_specs=[hbm] * 11,
+        out_specs=(hbm, vmem, vmem),
         scratch_shapes=[
+            *[pltpu.VMEM(array.shape, array.dtype) for array in (phases, energy, row_cell, col_cell, weight)],
+            *[pltpu.SMEM(array.shape, array.dtype) for array in (charge, pole_rate, pole_freq, pole_amp)],
             pltpu.VMEM((2, members, band, cols), F32),
             pltpu.VMEM((2, members, band, cols), F32),
             pltpu.VMEM(table.shape, BF16),
@@ -495,17 +541,17 @@
             pltpu.VMEM((groups, SUBLANES, lanes), F32),
             pltpu.VMEM((SUBLANES, lanes), F32),
             dma((members,)), dma((members,)), dma, dma, dma, dma, dma((members,)), dma((members,)),
-            dma((members,)), dma((members,)), dma((groups,)), dma((groups,)), dma((4,)),
+            dma((members,)), dma((members,)), dma((groups,)), dma((groups,)), dma((13,)),
         ],
         compiler_params=pltpu.CompilerParams(
-            collective_id=0, has_side_effects=True, vmem_limit_bytes=40 * 1024 * 1024
+            collective_id=0, has_side_effects=True, vmem_limit_bytes=64 * 1024 * 1024 - 64 * 1024
         ),
     )(field_in, phases, energy, row_cell, col_cell, weight, charge, pole_rate, pole_freq, pole_amp, table))
 
 
 def pick_plan(field_in, *others):
     members = field_in.shape[1]
-    whole = members == lax.axis_size("trans") and members >= 3 and lax.axis_size("beam") >= 3
+    whole = members == lax.axis_size("trans") and members % 2 == 0 and members >= 4 and lax.axis_size("beam") >= 3
     return (whole_slices if whole else shards)(field_in, *others)
 
 

time: 56 us -> 46.8 us (0.84)
  local copies, waits for them, and re-layouts: 11.1 us -> 3.4 us
  Pallas kernels: 43.7 us -> 42 us
    unnamed x25 -> x7, local copies, waits for them, and re-layouts: 11.1 us -> 3.4 us
    pallas_call x1, Pallas kernels: 43.7 us -> 42 us  [whole_slices(): pl.pallas_call(functools.partial(slices_kernel, groups), out_shape=(jax.S...]
where the time goes in v2:
time: 46.8 us; the launch traced here: 46.1 us
  Pallas kernels  42 us (90%)
  local copies, waits for them, and re-layouts  3.4 us (7%)
  between operations  0.65 us (1%)
    pallas_call x1, Pallas kernels, whole_slices(): pl.pallas_call(functools.partial(slices_kernel, groups), out_shape=(jax.S...  42 us
    unnamed x7, local copies, waits for them, and re-layouts  3.4 us

profile of v2, /device:TPU:0, one launch (start us, length us, event | category | flops | bytes accessed | tf_op | source)
XLA Modules:
  0.0 46.1 jit_solution(6618358317460704771)
XLA Ops:
  0.6 42.0 %shard_map.130 = (f32[2,4,64,256]{3,2,1,0:T(8,128)}, f32[4,4096]{1,0:T(4,128)}, f32[4,4096]{1,0:T(4,128)}) custom-call(f32[2,4,64,256]{3,2,1,0:T(8,128)} %field_in.1, f32[4,4096]{1,0:T(4,128)} %phases_in.1, f32[4,4096]{1,0:T(4,128)} %energy_in.1, s32[4,4096]{1,0:T(4,128)} %row_in.1, s32[4,4096]{1,0:T(4,128)} %col_in.1, s32[4,4096]{1,0:T(4,128)} %weight_in.1, ...), custom_call_target="tpu_custom_call" | custom-call | tf_op jit(solution)/shard_map/pallas_call | solution.py:517
  42.7 0.0 copy-start.1
  42.7 1.9 %copy.17 = f32[2,4,64,256]{3,2,1,0:T(8,128)} copy(f32[2,4,64,256]{3,2,1,0:T(8,128)} %get-tuple-element.6) | data formatting | bytes 1048576
  44.6 0.0 copy-done.1
  44.6 0.0 copy-start
  44.6 0.6 %copy.18 = f32[4,4096]{1,0:T(4,128)} copy(f32[4,4096]{1,0:T(4,128)S(1)} %copy-done.1) | data formatting | bytes 131072
  45.2 0.2 copy-done
  45.5 0.6 %copy.19 = f32[4,4096]{1,0:T(4,128)} copy(f32[4,4096]{1,0:T(4,128)S(1)} %copy-done) | data formatting | bytes 131072
Async XLA Ops:
  42.7 1.9 %copy-start.1 = (f32[4,4096]{1,0:T(4,128)S(1)}, f32[4,4096]{1,0:T(4,128)}, u32[]{:S(2)}) copy-start(f32[4,4096]{1,0:T(4,128)} %get-tuple-element.7) | copy-start | bytes 196612
  44.6 0.9 %copy-start = (f32[4,4096]{1,0:T(4,128)S(1)}, f32[4,4096]{1,0:T(4,128)}, u32[]{:S(2)}) copy-start(f32[4,4096]{1,0:T(4,128)} %get-tuple-element.8) | copy-start | bytes 196612

commit v3 on v2

--- a/solution.py
+++ b/solution.py
@@ -187,6 +187,7 @@
 MESH = pl.DeviceIdType.MESH
 LANES = 128
 SUBLANES = 8
+VMEM_GRANT = 64 * 1024 * 1024 - 64 * 1024
 F32 = jnp.float32
 BF16 = jnp.bfloat16
 
@@ -211,15 +212,11 @@
     return jnp.dot(left, right, preferred_element_type=F32)
 
 
-def mm_t(left, right):
-    return lax.dot_general(left, right, (((1,), (1,)), ((), ())), preferred_element_type=F32)
-
-
 def slices_kernel(
     groups,
     field_in, phases_in, energy_in, row_in, col_in, weight_in, charge_in, rate_in, freq_in, amp_in, table,
     field_out, phase_out, energy_out,
-    phases, energy, row_cell, col_cell, weight, charge, pole_rate, pole_freq, pole_amp, field, moved, taps, cells, state, result, arrived, probes, parts, halves, col_hot, row_hot, charges, charge_tile,
+    phases, energy, row_cell, col_cell, weight, charge, pole_rate, pole_freq, pole_amp, field, moved, taps, cells, state, result, arrived, probes, parts, halves, col_hot, col_hot_t, taps_t, row_hot, charges, charge_tile,
     field_send, field_recv, cell_send, cell_recv, state_send, state_recv, result_send, result_recv,
     out_send, out_recv, charge_send, charge_recv, local_sems,
 ):
@@ -275,9 +272,11 @@
 
     field_copies = []
     way = jnp.where(trans < half, 1, members - 1)
-    for step in [half] + [k for k in range(1, members) if k != half]:
-        to = lax.rem(trans + way * step, members)
-        copy = remote(field_in.at[:, to], field.at[:, trans], field_send.at[step], field_recv.at[trans], beam, to)
+    mine_half = trans // half
+    beyond = [(1 - mine_half) * half + lax.rem(trans + k, half) for k in range(half)]
+    nearby = [mine_half * half + lax.rem(trans + k, half) for k in range(1, half)]
+    for to in beyond + nearby:
+        copy = remote(field_in.at[:, to], field.at[:, trans], field_send.at[to], field_recv.at[trans], beam, to)
         copy.start()
         field_copies.append(copy)
 
@@ -312,7 +311,9 @@
         col_index = lax.broadcasted_iota(jnp.int32, (cols, width), 0).astype(F32)
 
         def body(k, carry):
-            col_hot[period, k] = jnp.where(cells[period, 1, pl.ds(k, 1), :] == col_index, 1.0, 0.0).astype(BF16)
+            hot = jnp.where(cells[period, 1, pl.ds(k, 1), :] == col_index, 1.0, 0.0)
+            col_hot[period, k] = hot.astype(BF16)
+            col_hot_t[period, k] = hot.T.astype(BF16)
             return carry
 
         lax.fori_loop(0, SUBLANES, body, 0)
@@ -394,7 +395,7 @@
                 [jnp.where(inside, parts[part, k : k + 1, :], 0.0).astype(BF16) for part in range(2)], axis=0
             )
             row_hot[:, k * width : (k + 1) * width] = spread
-            bunched = bunched + mm_t(row_hot[:, k * width : (k + 1) * width], col_hot[period, k])
+            bunched = bunched + mm(row_hot[:, k * width : (k + 1) * width], col_hot_t[period, k])
         strength = deposit_gain * wakes[period][1][:1, :1]
         flat = field[...].reshape(2, rows, cols)
         wide = []
@@ -402,7 +403,7 @@
             loaded = flat[part, edge : rows - edge] + strength * bunched[part * inner : (part + 1) * inner]
             wide.append(jnp.concatenate([flat[part, :edge], loaded, flat[part, rows - edge :]], axis=0))
         upper, lower = two_parts(jnp.concatenate(wide, axis=1))
-        across = mm_t(upper, taps[0]) + (mm_t(lower, taps[0]) + mm_t(upper, taps[1]))
+        across = mm(upper, taps_t[0]) + (mm(lower, taps_t[0]) + mm(upper, taps_t[1]))
         return two_parts(jnp.concatenate([across[:, :cols], across[:, cols:]], axis=0))
 
     def along_rows(first_row, count, upper, lower):
@@ -410,13 +411,17 @@
         major, minor = (jnp.concatenate([taps[part, where] for where in here], axis=0) for part in range(2))
         return (mm(major, upper) + (mm(major, lower) + mm(minor, upper))).reshape(2, count, cols)
 
+    take_table.wait()
+    for part in range(2):
+        both = taps[part]
+        taps_t[part, :cols] = jnp.concatenate([both[:cols, :cols], both[cols:, :cols]], axis=1)
+        taps_t[part, cols:] = jnp.concatenate([both[:cols, cols:], both[cols:, cols:]], axis=1)
     take.wait()
     probe_band(trans, True)
     for step in range(1, members):
         source = lax.rem(trans + way * step, members)
-        remote(field_in.at[:, source], field.at[:, source], field_send.at[step], field_recv.at[source], beam, source).wait_recv()
+        remote(field_in.at[:, source], field.at[:, source], field_send.at[source], field_recv.at[source], beam, source).wait_recv()
         probe_band(source, False)
-    take_table.wait()
     theta, eta = push(0, start_cos, start_sin)
     state[0, 0] = theta
     state[0, 1] = eta
@@ -483,7 +488,6 @@
     start_field, finish_field = scatter(
         2, lambda to: moved.at[:, to], lambda slot: field_out.at[:, slot], out_send, out_recv, local_sems.at[3]
     )
-    mine_half = trans // half
     for side in (1 - mine_half, mine_half):
         turned = along_rows(side * (half * band), half * band, upper, lower)
         turned = jnp.where(lax.rem(mine + 2, total) == 0, 0.0, turned)
@@ -500,6 +504,18 @@
     for copy in field_copies + charge_copies + [cell_copy, state_copy]:
         copy.wait_send()
     finish_field()
+
+
+def settle_kernel(field_made, phase_made, energy_made, field_out, phase_out, energy_out, sems):
+    pieces = [(phase_made, phase_out), (energy_made, energy_out)]
+    for part in range(2):
+        for place in range(field_made.shape[1]):
+            pieces.append((field_made.at[part, place], field_out.at[part, place]))
+    copies = [pltpu.make_async_copy(*piece, sems.at[k]) for k, piece in enumerate(pieces)]
+    for copy in copies:
+        copy.start()
+    for copy in copies:
+        copy.wait()
 
 
 def whole_slices(
@@ -514,7 +530,7 @@
     table = jnp.asarray(one_axis_propagator(cols))
     vmem, hbm = (pl.BlockSpec(memory_space=space) for space in (pltpu.VMEM, pltpu.HBM))
     dma = pltpu.SemaphoreType.DMA
-    return tuple(pl.pallas_call(
+    made = pl.pallas_call(
         functools.partial(slices_kernel, groups),
         out_shape=(
             jax.ShapeDtypeStruct(field_in.shape, F32),
@@ -537,6 +553,8 @@
             pltpu.VMEM((2, SUBLANES, width), F32),
             pltpu.VMEM((2, 2 * inner, cols), BF16),
             pltpu.VMEM((2, SUBLANES, cols, width), BF16),
+            pltpu.VMEM((2, SUBLANES, width, cols), BF16),
+            pltpu.VMEM(table.shape, BF16),
             pltpu.VMEM((2 * inner, SUBLANES * width), BF16),
             pltpu.VMEM((groups, SUBLANES, lanes), F32),
             pltpu.VMEM((SUBLANES, lanes), F32),
@@ -544,9 +562,18 @@
             dma((members,)), dma((members,)), dma((groups,)), dma((groups,)), dma((13,)),
         ],
         compiler_params=pltpu.CompilerParams(
-            collective_id=0, has_side_effects=True, vmem_limit_bytes=64 * 1024 * 1024 - 64 * 1024
+            collective_id=0, has_side_effects=True, vmem_limit_bytes=VMEM_GRANT
         ),
-    )(field_in, phases, energy, row_cell, col_cell, weight, charge, pole_rate, pole_freq, pole_amp, table))
+    )(field_in, phases, energy, row_cell, col_cell, weight, charge, pole_rate, pole_freq, pole_amp, table)
+    copies = 2 * members + 2
+    return tuple(pl.pallas_call(
+        settle_kernel,
+        out_shape=tuple(jax.ShapeDtypeStruct(array.shape, F32) for array in made),
+        in_specs=[hbm] * 3,
+        out_specs=(hbm,) * 3,
+        scratch_shapes=[dma((copies,))],
+        compiler_params=pltpu.CompilerParams(vmem_limit_bytes=VMEM_GRANT),
+    )(*made))
 
 
 def pick_plan(field_in, *others):

time: 46.8 us -> 65.3 us (1.40)
  Pallas kernels: 42 us -> 64 us
  local copies, waits for them, and re-layouts: 3.4 us -> 0 us
    pallas_call x0 -> x1, Pallas kernels: none -> 21 us  [whole_slices(): pl.pallas_call(settle_kernel, out_shape=tuple((jax.ShapeDtypeStruct(array...]
    unnamed x7 -> x0, local copies, waits for them, and re-layouts: 3.4 us -> none
    pallas_call x1, Pallas kernels: 42 us -> 42.9 us  [whole_slices(): pl.pallas_call(functools.partial(slices_kernel, groups), out_shape=(jax.S...]
where the time goes in v3:
time: 65.3 us; the launch traced here: 64.6 us
  Pallas kernels  64 us (98%)
    pallas_call x1, Pallas kernels, whole_slices(): pl.pallas_call(functools.partial(slices_kernel, groups), out_shape=(jax.S...  42.9 us
    pallas_call x1, Pallas kernels, whole_slices(): pl.pallas_call(settle_kernel, out_shape=tuple((jax.ShapeDtypeStruct(array...  21 us

profile of v3, /device:TPU:0, one launch (start us, length us, event | category | flops | bytes accessed | tf_op | source)
XLA Modules:
  0.0 64.6 jit_solution(5682541282289984783)
XLA Ops:
  0.6 42.9 %shard_map.130 = (f32[2,4,64,256]{3,2,1,0:T(8,128)}, f32[4,4096]{1,0:T(4,128)}, f32[4,4096]{1,0:T(4,128)}) custom-call(f32[2,4,64,256]{3,2,1,0:T(8,128)} %field_in.1, f32[4,4096]{1,0:T(4,128)} %phases_in.1, f32[4,4096]{1,0:T(4,128)} %energy_in.1, s32[4,4096]{1,0:T(4,128)} %row_in.1, s32[4,4096]{1,0:T(4,128)} %col_in.1, s32[4,4096]{1,0:T(4,128)} %weight_in.1, ...), custom_call_target="tpu_custom_call" | custom-call | tf_op jit(solution)/shard_map/pallas_call | solution.py:533
  43.6 21.0 %shard_map.131 = (f32[2,4,64,256]{3,2,1,0:T(8,128)}, f32[4,4096]{1,0:T(4,128)}, f32[4,4096]{1,0:T(4,128)}) custom-call(f32[2,4,64,256]{3,2,1,0:T(8,128)} %get-tuple-element.6.field_made, f32[4,4096]{1,0:T(4,128)} %get-tuple-element.7.phase_made, f32[4,4096]{1,0:T(4,128)} %get-tuple-element.8.energy_made), custom_call_target="tpu_custom_call" | custom-call | tf_op jit(solution)/shard_map/pallas_call | solution.py:569

commit v4 on v2

--- a/solution.py
+++ b/solution.py
@@ -187,6 +187,7 @@
 MESH = pl.DeviceIdType.MESH
 LANES = 128
 SUBLANES = 8
+VMEM_GRANT = 64 * 1024 * 1024 - 64 * 1024
 F32 = jnp.float32
 BF16 = jnp.bfloat16
 
@@ -219,7 +220,7 @@
     groups,
     field_in, phases_in, energy_in, row_in, col_in, weight_in, charge_in, rate_in, freq_in, amp_in, table,
     field_out, phase_out, energy_out,
-    phases, energy, row_cell, col_cell, weight, charge, pole_rate, pole_freq, pole_amp, field, moved, taps, cells, state, result, arrived, probes, parts, halves, col_hot, row_hot, charges, charge_tile,
+    phase_rows, energy_rows, phases, energy, row_cell, col_cell, weight, charge, pole_rate, pole_freq, pole_amp, field, moved, taps, cells, state, result, arrived, probes, parts, halves, col_hot, row_hot, charges, charge_tile,
     field_send, field_recv, cell_send, cell_recv, state_send, state_recv, result_send, result_recv,
     out_send, out_recv, charge_send, charge_recv, local_sems,
 ):
@@ -495,11 +496,37 @@
     for place in range(members):
         for k in range(SUBLANES):
             here = slice(k * width, (k + 1) * width)
-            phase_out[place : place + 1, here] = arrived[place, 0, k : k + 1, :]
-            energy_out[place : place + 1, here] = arrived[place, 1, k : k + 1, :]
+            phase_rows[place : place + 1, here] = arrived[place, 0, k : k + 1, :]
+            energy_rows[place : place + 1, here] = arrived[place, 1, k : k + 1, :]
+    leaving = [
+        pltpu.make_async_copy(phase_rows, phase_out, local_sems.at[13]),
+        pltpu.make_async_copy(energy_rows, energy_out, local_sems.at[14]),
+    ]
+    for copy in leaving:
+        copy.start()
     for copy in field_copies + charge_copies + [cell_copy, state_copy]:
         copy.wait_send()
     finish_field()
+    for copy in leaving:
+        copy.wait()
+
+
+def settle_kernel(
+    field_made, phase_made, energy_made, field_out, phase_out, energy_out, field, phase, energy, in_sems, out_sems
+):
+    pieces = [(phase_made, phase, phase_out), (energy_made, energy, energy_out)]
+    for part in range(2):
+        for place in range(field_made.shape[1]):
+            pieces.append(tuple(ref.at[part, place] for ref in (field_made, field, field_out)))
+    loads = [pltpu.make_async_copy(made, held, in_sems.at[k]) for k, (made, held, _) in enumerate(pieces)]
+    stores = [pltpu.make_async_copy(held, out, out_sems.at[k]) for k, (_, held, out) in enumerate(pieces)]
+    for load in loads:
+        load.start()
+    for load, store in zip(loads, stores):
+        load.wait()
+        store.start()
+    for store in stores:
+        store.wait()
 
 
 def whole_slices(
@@ -512,9 +539,9 @@
     width = phases.shape[1] // SUBLANES
     lanes = -(-groups * members // LANES) * LANES
     table = jnp.asarray(one_axis_propagator(cols))
-    vmem, hbm = (pl.BlockSpec(memory_space=space) for space in (pltpu.VMEM, pltpu.HBM))
+    hbm = pl.BlockSpec(memory_space=pltpu.HBM)
     dma = pltpu.SemaphoreType.DMA
-    return tuple(pl.pallas_call(
+    made = pl.pallas_call(
         functools.partial(slices_kernel, groups),
         out_shape=(
             jax.ShapeDtypeStruct(field_in.shape, F32),
@@ -522,9 +549,9 @@
             jax.ShapeDtypeStruct(energy.shape, F32),
         ),
         in_specs=[hbm] * 11,
-        out_specs=(hbm, vmem, vmem),
+        out_specs=(hbm,) * 3,
         scratch_shapes=[
-            *[pltpu.VMEM(array.shape, array.dtype) for array in (phases, energy, row_cell, col_cell, weight)],
+            *[pltpu.VMEM(array.shape, array.dtype) for array in (phases, energy, phases, energy, row_cell, col_cell, weight)],
             *[pltpu.SMEM(array.shape, array.dtype) for array in (charge, pole_rate, pole_freq, pole_amp)],
             pltpu.VMEM((2, members, band, cols), F32),
             pltpu.VMEM((2, members, band, cols), F32),
@@ -541,12 +568,21 @@
             pltpu.VMEM((groups, SUBLANES, lanes), F32),
             pltpu.VMEM((SUBLANES, lanes), F32),
             dma((members,)), dma((members,)), dma, dma, dma, dma, dma((members,)), dma((members,)),
-            dma((members,)), dma((members,)), dma((groups,)), dma((groups,)), dma((13,)),
+            dma((members,)), dma((members,)), dma((groups,)), dma((groups,)), dma((15,)),
         ],
         compiler_params=pltpu.CompilerParams(
-            collective_id=0, has_side_effects=True, vmem_limit_bytes=64 * 1024 * 1024 - 64 * 1024
+            collective_id=0, has_side_effects=True, vmem_limit_bytes=VMEM_GRANT
         ),
-    )(field_in, phases, energy, row_cell, col_cell, weight, charge, pole_rate, pole_freq, pole_amp, table))
+    )(field_in, phases, energy, row_cell, col_cell, weight, charge, pole_rate, pole_freq, pole_amp, table)
+    copies = 2 * members + 2
+    return tuple(pl.pallas_call(
+        settle_kernel,
+        out_shape=tuple(jax.ShapeDtypeStruct(array.shape, F32) for array in made),
+        in_specs=[hbm] * 3,
+        out_specs=(hbm,) * 3,
+        scratch_shapes=[*[pltpu.VMEM(array.shape, F32) for array in made], dma((copies,)), dma((copies,))],
+        compiler_params=pltpu.CompilerParams(vmem_limit_bytes=VMEM_GRANT),
+    )(*made))
 
 
 def pick_plan(field_in, *others):

time: 46.8 us -> 44.7 us (0.955)
  local copies, waits for them, and re-layouts: 3.4 us -> 0 us
  Pallas kernels: 42 us -> 43.3 us
    unnamed x7 -> x0, local copies, waits for them, and re-layouts: 3.4 us -> none
    pallas_call x0 -> x1, Pallas kernels: none -> 1.92 us  [whole_slices(): pl.pallas_call(settle_kernel, out_shape=tuple((jax.ShapeDtypeStruct(array...]
    pallas_call x1, Pallas kernels: 42 us -> 41.4 us  [whole_slices(): pl.pallas_call(functools.partial(slices_kernel, groups), out_shape=(jax.S...]
where the time goes in v4:
time: 44.7 us; the launch traced here: 44 us
  Pallas kernels  43.3 us (97%)
  between operations  0.64 us (1%)
    pallas_call x1, Pallas kernels, whole_slices(): pl.pallas_call(functools.partial(slices_kernel, groups), out_shape=(jax.S...  41.4 us
    pallas_call x1, Pallas kernels, whole_slices(): pl.pallas_call(settle_kernel, out_shape=tuple((jax.ShapeDtypeStruct(array...  1.92 us

profile of v4, /device:TPU:0, one launch (start us, length us, event | category | flops | bytes accessed | tf_op | source)
XLA Modules:
  0.0 44.0 jit_solution(2619879938396232141)
XLA Ops:
  0.6 41.4 %shard_map.130 = (f32[2,4,64,256]{3,2,1,0:T(8,128)}, f32[4,4096]{1,0:T(4,128)}, f32[4,4096]{1,0:T(4,128)}) custom-call(f32[2,4,64,256]{3,2,1,0:T(8,128)} %field_in.1, f32[4,4096]{1,0:T(4,128)} %phases_in.1, f32[4,4096]{1,0:T(4,128)} %energy_in.1, s32[4,4096]{1,0:T(4,128)} %row_in.1, s32[4,4096]{1,0:T(4,128)} %col_in.1, s32[4,4096]{1,0:T(4,128)} %weight_in.1, ...), custom_call_target="tpu_custom_call" | custom-call | tf_op jit(solution)/shard_map/pallas_call | solution.py:544
  42.0 1.9 %shard_map.131 = (f32[2,4,64,256]{3,2,1,0:T(8,128)}, f32[4,4096]{1,0:T(4,128)}, f32[4,4096]{1,0:T(4,128)}) custom-call(f32[2,4,64,256]{3,2,1,0:T(8,128)} %get-tuple-element.6.field_made, f32[4,4096]{1,0:T(4,128)} %get-tuple-element.7.phase_made, f32[4,4096]{1,0:T(4,128)} %get-tuple-element.8.energy_made), custom_call_target="tpu_custom_call" | custom-call | tf_op jit(solution)/shard_map/pallas_call | solution.py:578

commit v5 on v4

--- a/solution.py
+++ b/solution.py
@@ -220,7 +220,7 @@
     groups,
     field_in, phases_in, energy_in, row_in, col_in, weight_in, charge_in, rate_in, freq_in, amp_in, table,
     field_out, phase_out, energy_out,
-    phase_rows, energy_rows, phases, energy, row_cell, col_cell, weight, charge, pole_rate, pole_freq, pole_amp, field, moved, taps, cells, state, result, arrived, probes, parts, halves, col_hot, row_hot, charges, charge_tile,
+    phase_rows, energy_rows, phases, energy, row_cell, col_cell, weight, charge, pole_rate, pole_freq, pole_amp, field, moved, taps, cells, state, result, arrived, probes, parts, halves, col_hot, taps_t, row_hot, charges, charge_tile,
     field_send, field_recv, cell_send, cell_recv, state_send, state_recv, result_send, result_recv,
     out_send, out_recv, charge_send, charge_recv, local_sems,
 ):
@@ -276,9 +276,11 @@
 
     field_copies = []
     way = jnp.where(trans < half, 1, members - 1)
-    for step in [half] + [k for k in range(1, members) if k != half]:
-        to = lax.rem(trans + way * step, members)
-        copy = remote(field_in.at[:, to], field.at[:, trans], field_send.at[step], field_recv.at[trans], beam, to)
+    mine_half = trans // half
+    beyond = [(1 - mine_half) * half + lax.rem(trans + k, half) for k in range(half)]
+    nearby = [mine_half * half + lax.rem(trans + k, half) for k in range(1, half)]
+    for to in beyond + nearby:
+        copy = remote(field_in.at[:, to], field.at[:, trans], field_send.at[to], field_recv.at[trans], beam, to)
         copy.start()
         field_copies.append(copy)
 
@@ -403,7 +405,7 @@
             loaded = flat[part, edge : rows - edge] + strength * bunched[part * inner : (part + 1) * inner]
             wide.append(jnp.concatenate([flat[part, :edge], loaded, flat[part, rows - edge :]], axis=0))
         upper, lower = two_parts(jnp.concatenate(wide, axis=1))
-        across = mm_t(upper, taps[0]) + (mm_t(lower, taps[0]) + mm_t(upper, taps[1]))
+        across = mm(upper, taps_t[0]) + (mm(lower, taps_t[0]) + mm(upper, taps_t[1]))
         return two_parts(jnp.concatenate([across[:, :cols], across[:, cols:]], axis=0))
 
     def along_rows(first_row, count, upper, lower):
@@ -411,13 +413,17 @@
         major, minor = (jnp.concatenate([taps[part, where] for where in here], axis=0) for part in range(2))
         return (mm(major, upper) + (mm(major, lower) + mm(minor, upper))).reshape(2, count, cols)
 
+    take_table.wait()
+    for part in range(2):
+        both = taps[part]
+        taps_t[part, :cols] = jnp.concatenate([both[:cols, :cols], both[cols:, :cols]], axis=1)
+        taps_t[part, cols:] = jnp.concatenate([both[:cols, cols:], both[cols:, cols:]], axis=1)
     take.wait()
     probe_band(trans, True)
     for step in range(1, members):
         source = lax.rem(trans + way * step, members)
-        remote(field_in.at[:, source], field.at[:, source], field_send.at[step], field_recv.at[source], beam, source).wait_recv()
+        remote(field_in.at[:, source], field.at[:, source], field_send.at[source], field_recv.at[source], beam, source).wait_recv()
         probe_band(source, False)
-    take_table.wait()
     theta, eta = push(0, start_cos, start_sin)
     state[0, 0] = theta
     state[0, 1] = eta
@@ -484,7 +490,6 @@
     start_field, finish_field = scatter(
         2, lambda to: moved.at[:, to], lambda slot: field_out.at[:, slot], out_send, out_recv, local_sems.at[3]
     )
-    mine_half = trans // half
     for side in (1 - mine_half, mine_half):
         turned = along_rows(side * (half * band), half * band, upper, lower)
         turned = jnp.where(lax.rem(mine + 2, total) == 0, 0.0, turned)
@@ -564,6 +569,7 @@
             pltpu.VMEM((2, SUBLANES, width), F32),
             pltpu.VMEM((2, 2 * inner, cols), BF16),
             pltpu.VMEM((2, SUBLANES, cols, width), BF16),
+            pltpu.VMEM(table.shape, BF16),
             pltpu.VMEM((2 * inner, SUBLANES * width), BF16),
             pltpu.VMEM((groups, SUBLANES, lanes), F32),
             pltpu.VMEM((SUBLANES, lanes), F32),

time: 44.7 us -> 44.8 us (level)
  no operation moved by 1% of the time
where the time goes in v5:
time: 44.8 us; the launch traced here: 44.2 us
  Pallas kernels  43.5 us (97%)
  between operations  0.64 us (1%)
    pallas_call x1, Pallas kernels, whole_slices(): pl.pallas_call(functools.partial(slices_kernel, groups), out_shape=(jax.S...  41.6 us
    pallas_call x1, Pallas kernels, whole_slices(): pl.pallas_call(settle_kernel, out_shape=tuple((jax.ShapeDtypeStruct(array...  1.92 us

profile of v5, /device:TPU:0, one launch (start us, length us, event | category | flops | bytes accessed | tf_op | source)
XLA Modules:
  0.0 44.2 jit_solution(10041303289169952283)
XLA Ops:
  0.6 41.6 %shard_map.130 = (f32[2,4,64,256]{3,2,1,0:T(8,128)}, f32[4,4096]{1,0:T(4,128)}, f32[4,4096]{1,0:T(4,128)}) custom-call(f32[2,4,64,256]{3,2,1,0:T(8,128)} %field_in.1, f32[4,4096]{1,0:T(4,128)} %phases_in.1, f32[4,4096]{1,0:T(4,128)} %energy_in.1, s32[4,4096]{1,0:T(4,128)} %row_in.1, s32[4,4096]{1,0:T(4,128)} %col_in.1, s32[4,4096]{1,0:T(4,128)} %weight_in.1, ...), custom_call_target="tpu_custom_call" | custom-call | tf_op jit(solution)/shard_map/pallas_call | solution.py:549
  42.2 1.9 %shard_map.131 = (f32[2,4,64,256]{3,2,1,0:T(8,128)}, f32[4,4096]{1,0:T(4,128)}, f32[4,4096]{1,0:T(4,128)}) custom-call(f32[2,4,64,256]{3,2,1,0:T(8,128)} %get-tuple-element.6.field_made, f32[4,4096]{1,0:T(4,128)} %get-tuple-element.7.phase_made, f32[4,4096]{1,0:T(4,128)} %get-tuple-element.8.energy_made), custom_call_target="tpu_custom_call" | custom-call | tf_op jit(solution)/shard_map/pallas_call | solution.py:584
